TPU v7x, 1024 devices: a whole 4x8x16 slice. The times are simulated.
1024 devices in a mesh: dp: 256 (over y_hi, z, x), head: 4 (over y_lo, core).
Axes of the slice: x: 4, y: 8 (y_hi: 4, y_lo: 2; y = y_hi * 2 + y_lo), z: 16, core: 2. Of those that a mesh axis runs over, the one named last changes fastest.
Arguments:
- q_cot: bfloat16 [65536, 6144], P('dp', 'head'), may hold values from -6 to 6
- k_cot: bfloat16 [65536, 4096], P('dp', 'head'), may hold values from -6 to 6
- q_latent: bfloat16 [65536, 1536], P('dp'), may hold values from -240 to 240
- q_gain: float32 [1536], replicated, may hold values from 0.1 to 1.9
- w_uq: bfloat16 [1536, 6144], P('dp', 'head'), may hold values from -0.15625 to 0.15625
- w_uk: bfloat16 [512, 4096], P('dp', 'head'), may hold values from -0.25 to 0.25
Outputs:
- d_query: bfloat16 [65536, 1536], P('dp', 'head')
- d_latent: bfloat16 [65536, 512], P('dp', 'head')
All inputs are finite; a program needn't handle non-finite values.
Results may differ from a plain program's by a relative error of at most 0.0012.
Values may be sent and summed in bfloat16 or wider, within the bound.
A program may use at most 32 MiB of HBM per device.

v0:
```python
import jax
import jax.numpy as jnp
from jax import lax
from jax.sharding import PartitionSpec as P

norm_eps = 1e-06


def contract_rows(left_side, weight_piece):
    return lax.dot_general(
        left_side, weight_piece, (((1,), (1,)), ((), ())), preferred_element_type=jnp.float32
    )


def on_device(q_cot, k_cot, q_latent, q_gain, w_uq, w_uk):
    key_part = contract_rows(k_cot, lax.all_gather(w_uk, "dp", axis=0, tiled=True))
    query_part = contract_rows(q_cot, lax.all_gather(w_uq, "dp", axis=0, tiled=True))
    latent_float = q_latent.astype(jnp.float32)
    root_mean = jnp.sqrt(jnp.mean(latent_float * latent_float, axis=1, keepdims=True) + norm_eps)
    head_index = lax.axis_index("head")
    share_width = latent_float.shape[1] // lax.axis_size("head")
    d_latent = lax.psum_scatter(key_part, "head", scatter_dimension=1, tiled=True)
    d_normed = lax.psum(query_part, "head")
    normed = latent_float / root_mean
    scaled = q_gain[None, :] * d_normed
    row_dot = jnp.mean(scaled * normed, axis=1, keepdims=True)
    full_rows = (scaled - normed * row_dot) / root_mean
    d_query = lax.dynamic_slice_in_dim(full_rows, head_index * share_width, share_width, 1)
    return (d_query.astype(jnp.bfloat16), d_latent.astype(jnp.bfloat16))


def solution(mesh):
    return jax.shard_map(
        on_device,
        mesh=mesh,
        in_specs=(
            P("dp", "head"),
            P("dp", "head"),
            P("dp", None),
            P(),
            P("dp", "head"),
            P("dp", "head"),
        ),
        out_specs=(P("dp", "head"), P("dp", "head")),
        check_vma=False,
    )
```

profile of v0, /device:TPU:1, one launch (start us, length us, event | category | flops | bytes accessed | tf_op | source)
XLA Modules:
  0.0 569.8 jit_solution(3958613971039534773)
XLA Ops:
  7.2 0.0 copy-start
  7.2 0.0 copy-start.2
  7.2 0.0 all-gather.7.cloned.1.call-start
  7.2 0.7 all-gather.7.cloned.1.call-update
  7.9 0.0 all-gather.5.cloned.1.call-start
  8.0 0.7 all-gather.5.cloned.1.call-update
  8.7 0.0 reduce-scatter.2.cloned.1.call-start
  8.7 205.7 %all-gather.7.cloned.1.call-done = bf16[256,2,1024]{2,1,0:T(2,128)(2,1)} async-done(((bf16[1,2,1024]{2,1,0:T(2,128)(2,1)}), bf16[256,2,1024]{2,1,0:T(2,128)(2,1)}) %all-gather.7.cloned.1.call-update) | async-done | bytes 1048592 | tf_op jit(solution)/shard_map/all_gather | solution.py:16
  214.4 1.5 reshape.20
  215.9 0.0 copy-done.2
  215.9 1.3 fusion.4
  217.2 0.0 reduce-scatter.2.cloned.1.call-update
  217.2 0.0 all-reduce.2.cloned.1.call-start
  217.2 233.2 %all-gather.5.cloned.1.call-done = bf16[256,6,1536]{2,1,0:T(8,128)(2,1)} async-done(((bf16[1,6,1536]{2,1,0:T(8,128)(2,1)}), bf16[256,6,1536]{2,1,0:T(8,128)(2,1)}) %all-gather.5.cloned.1.call-update) | async-done | bytes 4718608 | tf_op jit(solution)/shard_map/all_gather | solution.py:17
  450.4 8.4 %reshape.18 = bf16[1536,1536]{1,0:T(8,128)(2,1)} reshape(bf16[256,6,1536]{2,1,0:T(8,128)(2,1)} %all-gather.5.cloned.1.call-done) | data formatting | bytes 9437184
  458.8 0.0 copy-done
  458.9 4.9 fusion.3
  463.8 0.0 copy-start.1
  463.8 0.0 copy-start.3
  463.8 0.0 all-reduce.2.cloned.1.call-update
  463.8 1.1 copy-done.1
  464.9 0.2 fusion
  465.1 22.2 %reduce-scatter.2.cloned.1.call-done = f32[256,128]{1,0:T(8,128)} async-done(((f32[256,512]{1,0:T(8,128)}), f32[256,128]{1,0:T(8,128)}) %reduce-scatter.2.cloned.1.call-update) | async-done | bytes 131088 | tf_op jit(solution)/shard_map/reduce_scatter | solution.py:22
  487.3 1.5 convert_element_type.11
  488.8 71.8 %all-reduce.2.cloned.1.call-done = f32[256,1536]{1,0:T(8,128)} async-done(((f32[256,1536]{1,0:T(8,128)}), f32[256,1536]{1,0:T(8,128)}) %all-reduce.2.cloned.1.call-update) | async-done | bytes 1572880 | tf_op jit(solution)/shard_map/psum | solution.py:23
  560.6 0.0 copy-done.3
  560.6 1.8 multiply_reduce_fusion
  562.4 0.8 fusion.2
  (2 shorter events, 0.0 us)
Async XLA Ops:
  7.2 451.7 %copy-start = (bf16[256,1536]{1,0:T(8,128)(2,1)S(1)}, bf16[256,1536]{1,0:T(8,128)(2,1)}, u32[]{:S(2)}) copy-start(bf16[256,1536]{1,0:T(8,128)(2,1)} %param.6) | copy-start | bytes 2359300
  7.2 208.7 %copy-start.2 = (bf16[256,1024]{1,0:T(8,128)(2,1)S(1)}, bf16[256,1024]{1,0:T(8,128)(2,1)}, u32[]{:S(2)}) copy-start(bf16[256,1024]{1,0:T(8,128)(2,1)} %param.7) | copy-start | bytes 1572868
  7.2 207.2 %all-gather.7.cloned.1.call-start = ((), (), s32[]{:S(2)}) async-start(), calls=%async_computation.4 | async-start | bytes 1052672 | tf_op jit(solution)/shard_map/all_gather | solution.py:16
  7.9 442.5 %all-gather.5.cloned.1.call-start = ((), (), s32[]{:S(2)}) async-start(), calls=%async_computation.3 | async-start | bytes 6316032 | tf_op jit(solution)/shard_map/all_gather | solution.py:17
  8.7 478.6 %reduce-scatter.2.cloned.1.call-start = ((), (), s32[]{:S(2)}) async-start(), calls=%async_computation.2 | async-start | bytes 655360 | tf_op jit(solution)/shard_map/reduce_scatter | solution.py:22
  217.2 343.4 %all-reduce.2.cloned.1.call-start = ((), (), s32[]{:S(2)}) async-start(), calls=%async_computation.1 | async-start | bytes 3145728 | tf_op jit(solution)/shard_map/psum | solution.py:23
  463.8 1.1 copy-start.1
  463.8 96.8 %copy-start.3 = (f32[1536]{0:T(1024)S(1)}, f32[1536]{0:T(1024)}, u32[]{:S(2)}) copy-start(f32[1536]{0:T(1024)} %param.9) | copy-start | bytes 18436
Sparse Core Ops, SparseCore 0:
  13.8 200.5 all-gather.6
  220.2 230.1 all-gather.4
  453.8 33.4 reduce-scatter.1
  490.7 69.8 all-reduce.1
where the time goes:
time: 570 us
  waiting for transfers between devices  534 us (94%)
  between operations  13.8 us (2%)
  local copies, waits for them, and re-layouts  11 us (2%)
  matrix products  6.18 us (1%)
    all_gather x1, waiting for transfers between devices, on_device(): lax.all_gather(w_uq, 'dp', axis=0, tiled=True)  233 us
    all_gather x1, waiting for transfers between devices, on_device(): lax.all_gather(w_uk, 'dp', axis=0, tiled=True)  206 us
    psum x1, waiting for transfers between devices, on_device(): d_normed = lax.psum(query_part, 'head')  71.8 us
    reduce_scatter x1, waiting for transfers between devices, on_device(): lax.psum_scatter(key_part, 'head', scatter_dimension=1, tiled=True)  22.2 us
  transfers between devices with their start and end apart: 4, of which 4 were waited for; matrix products, arithmetic and copies ran while one was open for 3% of the time, Pallas kernels for 0%

commit v1 on v0

v1 whole, which is shorter than its diff:
```python
import jax
import jax.numpy as jnp
from jax import lax
from jax.experimental import pallas as pl
from jax.experimental.pallas import tpu as pltpu
from jax.sharding import PartitionSpec as P

norm_eps = 1e-06
MESH = pl.DeviceIdType.MESH

NX, NZ, NYH = 4, 16, 4
TOK, QR, KVR = 256, 1536, 512
QF, KF = 1536, 1024
WIDE = 2 * QF
C1 = 1024
C2 = WIDE - C1
J1 = 2
P1 = C1 // J1
HALF = C2 // 2
SHARE = QR // 4
LSHARE = KVR // 4


def kernel(
    q_cot, k_cot, q_lat_hbm, gain, w_uq, w_uk, d_query, d_latent,
    a_all, w1, w2, y_land, y_send, stage, q_lat, root, gain_normed, products,
    part, part_in, dot_mine, dot_in,
    local_sem, a_send, a_recv, y_ssem, y_rsem, x1_send, x1_recv,
    z1_send, z1_recv, z2_send, z2_recv, x2_send, x2_first, x2_rest, fwd_send,
    part_send, part_recv, dot_send, dot_recv,
):
    dp, head = lax.axis_index("dp"), lax.axis_index("head")
    x, z, yh = dp % NX, (dp // NX) % NZ, dp // (NX * NZ)
    ylo, core = head // 2, head % 2

    def at(nyh, nz, nx, nylo, ncore):
        return ((nyh * NZ + nz) * NX + nx, nylo * 2 + ncore)

    xr, xl, xo = (x + 1) % NX, (x + NX - 1) % NX, (x + 2) % NX
    zr, zl = (z + 1) % NZ, (z + NZ - 1) % NZ
    sibling = at(yh, z, x, ylo, 1 - core)
    facing = at(yh, z, x, 1 - ylo, core)
    facing_sibling = at(yh, z, x, 1 - ylo, 1 - core)
    to_x = (at(yh, z, xr, ylo, core), at(yh, z, xl, ylo, core))
    to_x_over = at(yh, z, xo, ylo, core)
    to_z = (at(yh, zr, x, ylo, core), at(yh, zl, x, ylo, core))

    def remote(src, dst, ssem, rsem, device):
        return pltpu.make_async_remote_copy(
            src_ref=src, dst_ref=dst, send_sem=ssem, recv_sem=rsem,
            device_id=device, device_id_type=MESH,
        )

    own_q = pltpu.make_async_copy(q_cot, a_all.at[core, pl.ds(0, TOK)], local_sem.at[0])
    own_k = [
        pltpu.make_async_copy(
            k_cot.at[:, pl.ds(h * 512, 512)],
            a_all.at[core, pl.ds(TOK, TOK), pl.ds(h * 768, 512)],
            local_sem.at[1 + h],
        )
        for h in range(2)
    ]
    own_lat = pltpu.make_async_copy(q_lat_hbm, q_lat, local_sem.at[3])
    own_lat.start()
    own_q.start()
    for copy in own_k:
        copy.start()

    barrier = pltpu.get_barrier_semaphore()
    partners = [to_x[0], to_x[1], to_x_over, to_z[0], to_z[1], facing, facing_sibling, sibling]
    for j in range(1, NYH):
        for c in range(2):
            partners.append(at((yh + j) % NYH, z, x, ylo, c))
    for device in partners:
        pl.semaphore_signal(barrier, inc=1, device_id=device, device_id_type=MESH)

    uq = w_uq[...].astype(jnp.float32)
    uk = w_uk[...].astype(jnp.float32)
    for h in range(2):
        stage[8 * h : 8 * h + 6, 0:768] = uq[:, h * 768 : (h + 1) * 768]
        stage[8 * h + 6 : 8 * h + 8, 0:512] = uk[:, h * 512 : (h + 1) * 512]
        stage[8 * h + 6 : 8 * h + 8, 512:768] = jnp.zeros((2, 256), jnp.float32)
    y_send[...] = stage[:, 0:768].astype(jnp.bfloat16)

    pl.semaphore_wait(barrier, len(partners))

    y_core, y_half = yh % 2, yh // 2
    for j in range(NYH):
        stays = jnp.logical_and(yh == j, y_core == core)

        @pl.when(jnp.logical_not(stays))
        def _(j=j):
            remote(
                y_send, y_land.at[y_half, core], y_ssem.at[j], y_rsem.at[y_half, core],
                at(j, z, x, ylo, y_core),
            ).start()

    mine = y_core == core

    @pl.when(mine)
    def _():
        y_land[y_half, core] = y_send[...]

    give_q = remote(
        q_cot, a_all.at[core, pl.ds(0, TOK)], a_send.at[0], a_recv.at[0], sibling
    )
    give_k = [
        remote(
            k_cot.at[:, pl.ds(h * 512, 512)],
            a_all.at[core, pl.ds(TOK, TOK), pl.ds(h * 768, 512)],
            a_send.at[1 + h], a_recv.at[1 + h], sibling,
        )
        for h in range(2)
    ]
    give_q.start()
    for copy in give_k:
        copy.start()

    for c in range(2):
        for h in range(2):
            a_all[c, TOK : 2 * TOK, h * 768 + 512 : (h + 1) * 768] = jnp.zeros((TOK, 256), jnp.bfloat16)

    for half in range(2):
        for c in range(2):
            source_yh = core + 2 * half
            local = jnp.logical_and(source_yh == yh, core == c)

            @pl.when(jnp.logical_not(local))
            def _(half=half, c=c, source_yh=source_yh):
                remote(
                    y_send, y_land.at[half, c], y_ssem.at[0], y_rsem.at[half, c],
                    at((yh + 1) % NYH, z, x, ylo, c),
                ).wait_recv()

            piece = y_land[half, c].astype(jnp.float32)
            for h in range(2):
                columns = slice(c * QF + h * 768, c * QF + (h + 1) * 768)
                stage[6 * half : 6 * half + 6, columns] = piece[8 * h : 8 * h + 6]
                stage[12 + 2 * half : 14 + 2 * half, columns] = piece[8 * h + 6 : 8 * h + 8]

    def rows_of(nx):
        return pl.ds(pl.multiple_of(nx * 16, 16), 16)

    w1[z, rows_of(x), :] = stage[:, 0:C1].astype(jnp.bfloat16)
    w2[z, rows_of(x), :] = stage[:, C1:WIDE].astype(jnp.bfloat16)

    def ring2(way, block):
        src = w2.at[block, rows_of(x)]
        return remote(src, src, z2_send.at[0], z2_recv.at[block], to_z[way])

    def cross(way, block, half, first):
        src = w2.at[block, rows_of(x), pl.ds(half * HALF, HALF)]
        sem = x2_first.at[way, block] if first else x2_rest.at[block]
        return remote(src, src, x2_send.at[0], sem, to_x[way])

    def start_cross(block):
        for way in range(2):
            cross(way, block, way, True).start()
        for way in range(2):
            cross(way, block, 1 - way, False).start()

    def ring1(way, block, j):
        src = w1.at[block, :, pl.ds(j * P1, P1)]
        return remote(src, src, z1_send.at[0], z1_recv.at[block, j], to_z[way])

    ring2(0, z).start()
    ring2(1, z).start()
    src1 = w1.at[z, rows_of(x)]
    for k, device in enumerate((to_x[0], to_x[1], to_x_over)):
        remote(src1, src1, x1_send.at[0], x1_recv.at[x], device).start()
    start_cross(z)

    own_lat.wait()
    latent = q_lat[...].astype(jnp.float32)
    root_mean = jnp.sqrt(jnp.mean(latent * latent, axis=1, keepdims=True) + norm_eps)
    root[...] = jnp.broadcast_to(root_mean, (TOK, 128))
    for half in range(2):
        columns = pl.ds(pl.multiple_of((core + 2 * half) * SHARE, 128), SHARE)
        normed = q_lat[:, columns].astype(jnp.float32) / root_mean
        gain_normed[half] = (gain[:, columns] * normed).T
    dot_mine[...] = jnp.zeros_like(dot_mine)

    for k in range(1, NX):
        nx = (x + k) % NX
        dst = w1.at[z, rows_of(nx)]
        remote(dst, dst, x1_send.at[0], x1_recv.at[nx], to_x_over).wait_recv()
    for j in range(J1):
        ring1(0, z, j).start()
        ring1(1, z, j).start()

    own_q.wait()
    give_q.wait_recv()
    for h in range(2):
        own_k[h].wait()
        give_k[h].wait_recv()

    def multiply(block_a, block_b):
        total = None
        for t in range(WIDE // 512):
            ref, start = (w1, t * 512) if t * 512 < C1 else (w2, t * 512 - C1)
            left = jnp.concatenate(
                [ref[block_a, :, start : start + 512], ref[block_b, :, start : start + 512]], axis=0
            )
            c, a_start = t * 512 // QF, t * 512 % QF
            term = lax.dot_general(
                left, a_all[c, :, a_start : a_start + 512], (((1,), (1,)), ((), ())),
                preferred_element_type=jnp.float32,
            )
            total = term if total is None else total + term
        products[...] = total
        dot = dot_mine[...]
        for g, block in enumerate((block_a, block_b)):
            for half in range(2):
                for nx in range(NX):
                    base = g * 64 + nx * 16
                    part[half, block, 6 * nx : 6 * nx + 6, :] = products[
                        base + 6 * half : base + 6 * half + 6, 0:TOK
                    ]
                    part[half, block, 24 + 2 * nx : 26 + 2 * nx, :] = products[
                        base + 12 + 2 * half : base + 14 + 2 * half, TOK : 2 * TOK
                    ]
            send_part(block).start()
            for half in range(2):
                weighted = (
                    part[half, block, 0:24, :]
                    * gain_normed[half, pl.ds(pl.multiple_of(block * 24, 8), 24), :]
                )
                dot = dot + (weighted[0:8] + weighted[8:16] + weighted[16:24])
        dot_mine[...] = dot

    def send_part(block):
        return remote(
            part.at[1 - ylo, block], part_in.at[block], part_send.at[0], part_recv.at[block], facing
        )

    def step(s, carry):
        behind, ahead = (z - s + NZ) % NZ, (z + s) % NZ
        both = jnp.logical_and(s >= 1, s <= 7)

        @pl.when(jnp.logical_and(s >= 1, s <= 8))
        def _():
            ring2(0, behind).wait_recv()

            @pl.when(s < 8)
            def _():
                ring2(0, behind).start()

            @pl.when(s < 8)
            def _():
                ring2(1, ahead).wait_recv()

            @pl.when(s < 7)
            def _():
                ring2(1, ahead).start()

            start_cross(behind)

            @pl.when(s < 8)
            def _():
                start_cross(ahead)

            for j in range(J1):
                ring1(0, behind, j).wait_recv()

                @pl.when(s < 8)
                def _(j=j):
                    ring1(0, behind, j).start()

                @pl.when(s < 8)
                def _(j=j):
                    ring1(1, ahead, j).wait_recv()

                @pl.when(s < 7)
                def _(j=j):
                    ring1(1, ahead, j).start()

        def forward(block):
            for way, nx in ((0, xl), (1, xr)):
                src = w2.at[block, rows_of(nx), pl.ds(way * HALF, HALF)]
                remote(src, src, fwd_send.at[0], x2_first.at[way, block], to_x[way]).wait_recv()
                remote(src, src, fwd_send.at[0], x2_rest.at[block], to_x[way]).start()

        before, after = (z - s + 1 + NZ) % NZ, (z + s - 1) % NZ

        @pl.when(jnp.logical_and(s >= 1, s <= 9))
        def _():
            forward(before)

        @pl.when(jnp.logical_and(s >= 2, s <= 8))
        def _():
            forward(after)

        @pl.when(s >= 3)
        def _():
            p = s - 2
            block_a = (z - p + NZ) % NZ
            block_b = jnp.where(p == 8, z, (z + p) % NZ)
            for block in (block_a, block_b):
                dst = w2.at[block, :, pl.ds(0, HALF)]
                remote(dst, dst, x2_send.at[0], x2_rest.at[block], to_x[0]).wait_recv()
            multiply(block_a, block_b)

        return carry

    lax.fori_loop(1, 11, step, 0)

    dot_in[head] = dot_mine[...]
    for device in (facing, facing_sibling, sibling):
        remote(dot_mine, dot_in.at[head], dot_send.at[0], dot_recv.at[head], device).start()

    for j in range(NYH):
        stays = jnp.logical_and(yh == j, y_core == core)

        @pl.when(jnp.logical_not(stays))
        def _(j=j):
            remote(
                y_send, y_land.at[y_half, core], y_ssem.at[j], y_rsem.at[y_half, core],
                at(j, z, x, ylo, y_core),
            ).wait_send()

    give_q.wait_send()
    for copy in give_k:
        copy.wait_send()

    def sent(ref, sem):
        remote(ref, ref, sem.at[0], dot_recv.at[0], facing).wait_send()

    sent(w1.at[0, pl.ds(0, 48)], x1_send)
    sent(w1.at[pl.ds(0, NZ - 1)], z1_send)
    sent(w2.at[pl.ds(0, NZ - 1), pl.ds(0, 16)], z2_send)
    sent(w2.at[:, pl.ds(0, 32)], x2_send)
    sent(w2.at[:, pl.ds(0, 16)], fwd_send)

    for k in range(1, 4):
        other = (head + k) % 4
        remote(dot_mine, dot_in.at[other], dot_send.at[0], dot_recv.at[other], sibling).wait_recv()
    dots = dot_in[0] + dot_in[1] + dot_in[2] + dot_in[3]
    row_dot = jnp.sum(dots, axis=0, keepdims=True) / QR
    row_dot = jnp.broadcast_to(row_dot, (128, TOK)).T[:, 0:1]

    def arrived(block, carry):
        remote(
            part_in.at[block], part_in.at[block], part_send.at[0], part_recv.at[block], facing
        ).wait_recv()
        return carry

    lax.fori_loop(0, NZ, arrived, 0)
    whole = part[ylo] + part_in[...]
    d_normed = whole[:, 0:24, :].reshape(SHARE, TOK).T
    d_latent[...] = whole[:, 24:32, :].reshape(LSHARE, TOK).T.astype(jnp.bfloat16)
    columns = pl.ds(pl.multiple_of(head * SHARE, 128), SHARE)
    root_mean = root[:, 0:1]
    normed = q_lat[:, columns].astype(jnp.float32) / root_mean
    scaled = gain[:, columns] * d_normed
    d_query[...] = ((scaled - normed * row_dot) / root_mean).astype(jnp.bfloat16)
    sent(part_in, part_send)
    sent(dot_in.at[pl.ds(0, 3)], dot_send)


def on_device(q_cot, k_cot, q_latent, q_gain, w_uq, w_uk):
    vmem = pl.BlockSpec(memory_space=pltpu.VMEM)
    hbm = pl.BlockSpec(memory_space=pl.ANY)
    f32, bf16 = jnp.float32, jnp.bfloat16
    dma = pltpu.SemaphoreType.DMA
    return pl.pallas_call(
        kernel,
        out_shape=(
            jax.ShapeDtypeStruct((TOK, SHARE), bf16),
            jax.ShapeDtypeStruct((TOK, LSHARE), bf16),
        ),
        in_specs=[hbm, hbm, hbm, vmem, vmem, vmem],
        out_specs=(vmem, vmem),
        scratch_shapes=[
            pltpu.VMEM((2, 2 * TOK, QF), bf16),
            pltpu.VMEM((NZ, 64, C1), bf16),
            pltpu.VMEM((NZ, 64, C2), bf16),
            pltpu.VMEM((2, 2, 16, 768), bf16),
            pltpu.VMEM((16, 768), bf16),
            pltpu.VMEM((16, WIDE), f32),
            pltpu.VMEM((TOK, QR), bf16),
            pltpu.VMEM((TOK, 128), f32),
            pltpu.VMEM((2, SHARE, TOK), f32),
            pltpu.VMEM((128, 2 * TOK), f32),
            pltpu.VMEM((2, NZ, 32, TOK), f32),
            pltpu.VMEM((NZ, 32, TOK), f32),
            pltpu.VMEM((8, TOK), f32),
            pltpu.VMEM((4, 8, TOK), f32),
            dma((4,)),
            dma((3,)),
            dma((3,)),
            dma((4,)),
            dma((2, 2)),
            dma((1,)),
            dma((NX,)),
            dma((1,)),
            dma((NZ, J1)),
            dma((1,)),
            dma((NZ,)),
            dma((1,)),
            dma((2, NZ)),
            dma((NZ,)),
            dma((1,)),
            dma((1,)),
            dma((NZ,)),
            dma((1,)),
            dma((4,)),
        ],
        compiler_params=pltpu.CompilerParams(
            collective_id=0, has_side_effects=True, vmem_limit_bytes=40 * 2**20
        ),
        name="latent_backward",
    )(q_cot, k_cot, q_latent, q_gain.reshape(1, QR), w_uq, w_uk)


def solution(mesh):
    return jax.shard_map(
        on_device,
        mesh=mesh,
        in_specs=(
            P("dp", "head"),
            P("dp", "head"),
            P("dp", None),
            P(),
            P("dp", "head"),
            P("dp", "head"),
        ),
        out_specs=(P("dp", "head"), P("dp", "head")),
        check_vma=False,
    )
```

time: 570 us -> 85.2 us (0.15)
  waiting for transfers between devices: 534 us -> 0 us
  Pallas kernels: 0 us -> 78 us
  between operations: 13.8 us -> 0.65 us
  matrix products: 6.18 us -> 0 us
    all_gather x2 -> x0, waiting for transfers between devices: 439 us -> none  [the longest x1 233 us: on_device(): lax.all_gather(w_uq, 'dp', axis=0, tiled=True)]
    pallas_call x0 -> x1, Pallas kernels: none -> 78 us  [on_device(): pl.pallas_call(kernel, out_shape=(jax.ShapeDtypeStruct((TOK, SHARE), bf16...]
    psum x1 -> x0, waiting for transfers between devices: 71.8 us -> none  [on_device(): d_normed = lax.psum(query_part, 'head')]
    reduce_scatter x1 -> x0, waiting for transfers between devices: 22.2 us -> none  [on_device(): lax.psum_scatter(key_part, 'head', scatter_dimension=1, tiled=True)]
    dot_general x2 -> x0, matrix products: 6.18 us -> none  [contract_rows(): lax.dot_general(left_side, weight_piece, (((1,), (1,)), ((), ())), prefer...]
  transfers between devices with their start and end apart: 4 -> 0, of which waited for: 4 -> 0; matrix products, arithmetic and copies ran while one was open for 3% -> 0% of each run, Pallas kernels for 0% -> 0%
where the time goes in v1:
time: 85.2 us; the launch traced here: 84.7 us
  Pallas kernels  78 us (92%)
  local copies, waits for them, and re-layouts  6.06 us (7%)
    pallas_call x1, Pallas kernels, on_device(): pl.pallas_call(kernel, out_shape=(jax.ShapeDtypeStruct((TOK, SHARE), bf16...  78 us
    unnamed x12, local copies, waits for them, and re-layouts  5.35 us

profile of v1, /device:TPU:1, one launch (start us, length us, event | category | flops | bytes accessed | tf_op | source)
XLA Modules:
  0.0 84.7 jit_solution(9531846362652509569)
XLA Ops:
  0.6 0.0 copy-start.4
  0.6 0.7 reshape.7.gain
  1.3 0.0 copy-done.4
  1.4 0.0 copy-start
  1.4 1.1 %copy-done = bf16[256,1536]{1,0:T(8,128)(2,1)S(1)} copy-done((bf16[256,1536]{1,0:T(8,128)(2,1)S(1)}, bf16[256,1536]{1,0:T(8,128)(2,1)}, u32[]{:S(2)}) %copy-start) | copy-done | bytes 786456
  2.5 0.0 copy-start.1
  2.5 1.1 %copy-done.1 = bf16[256,1536]{1,0:T(8,128)(2,1)S(1)} copy-done((bf16[256,1536]{1,0:T(8,128)(2,1)S(1)}, bf16[256,1536]{1,0:T(8,128)(2,1)}, u32[]{:S(2)}) %copy-start.1) | copy-done | bytes 786456
  3.6 0.0 copy-start.2
  3.6 1.0 %copy-done.2 = bf16[256,1024]{1,0:T(8,128)(2,1)S(1)} copy-done((bf16[256,1024]{1,0:T(8,128)(2,1)S(1)}, bf16[256,1024]{1,0:T(8,128)(2,1)}, u32[]{:S(2)}) %copy-start.2) | copy-done | bytes 524312
  4.7 0.0 copy-start.3
  4.7 0.7 copy-done.3
  5.4 78.0 %latent_backward.1 = (bf16[256,384]{1,0:T(8,128)(2,1)S(1)}, bf16[256,128]{1,0:T(8,128)(2,1)S(1)}) custom-call(bf16[256,1536]{1,0:T(8,128)(2,1)S(1)} %copy-done, bf16[256,1024]{1,0:T(8,128)(2,1)S(1)} %copy-done.2, bf16[256,1536]{1,0:T(8,128)(2,1)S(1)} %copy-done.1, f32[1,1536]{1,0:T(1,128)S(1)} %reshape.7.gain, bf16[6,1536]{1,0:T(8,128)(2,1)S(1)} %copy-done.3, ...), custom_call_target="tpu_custom_call" | custom-call | tf_op jit(solution)/shard_map/latent_backward/pallas_call | solution.py:365
  83.4 0.7 copy.10
  84.1 0.6 copy.11
Async XLA Ops:
  0.6 0.7 copy-start.4
  1.4 1.1 %copy-start = (bf16[256,1536]{1,0:T(8,128)(2,1)S(1)}, bf16[256,1536]{1,0:T(8,128)(2,1)}, u32[]{:S(2)}) copy-start(bf16[256,1536]{1,0:T(8,128)(2,1)} %q_cot.1) | copy-start | bytes 2359300
  2.5 1.1 %copy-start.1 = (bf16[256,1536]{1,0:T(8,128)(2,1)S(1)}, bf16[256,1536]{1,0:T(8,128)(2,1)}, u32[]{:S(2)}) copy-start(bf16[256,1536]{1,0:T(8,128)(2,1)} %q_lat_hbm.1) | copy-start | bytes 2359300
  3.6 1.0 %copy-start.2 = (bf16[256,1024]{1,0:T(8,128)(2,1)S(1)}, bf16[256,1024]{1,0:T(8,128)(2,1)}, u32[]{:S(2)}) copy-start(bf16[256,1024]{1,0:T(8,128)(2,1)} %k_cot.1) | copy-start | bytes 1572868
  4.7 0.7 copy-start.3

commit v2 on v1

v2 whole, which is shorter than its diff:
```python
import jax
import jax.numpy as jnp
from jax import lax
from jax.experimental import pallas as pl
from jax.experimental.pallas import tpu as pltpu
from jax.sharding import PartitionSpec as P

norm_eps = 1e-06
MESH = pl.DeviceIdType.MESH

NX, NZ, NYH = 4, 16, 4
TOK, QR, KVR = 256, 1536, 512
QF, KF = 1536, 1024
C1 = 1024
C2 = 1792
HALF = C2 // 2
SHARE = QR // 4
LSHARE = KVR // 4


def kernel(
    q_cot, k_cot, q_lat_hbm, gain_flat, w_uq, w_uk, d_query, d_latent,
    a1, a2, w1, w2, y_land, y_send, stage1, stage2, q_lat, root, gain_normed, products,
    part, part_in, dot_mine, dot_in, gain,
    local_sem, a_send, a_recv, y_ssem, y_rsem, x1_send, x1_recv,
    z1_send, z1_recv, z2_send, z2_recv, x2_send, x2_first, x2_rest, fwd_send,
    part_send, part_recv, dot_send, dot_recv,
):
    dp, head = lax.axis_index("dp"), lax.axis_index("head")
    x, z, yh = dp % NX, (dp // NX) % NZ, dp // (NX * NZ)
    ylo, core = head // 2, head % 2

    def at(nyh, nz, nx, nylo, ncore):
        return ((nyh * NZ + nz) * NX + nx, nylo * 2 + ncore)

    xr, xl, xo = (x + 1) % NX, (x + NX - 1) % NX, (x + 2) % NX
    zr, zl = (z + 1) % NZ, (z + NZ - 1) % NZ
    sibling = at(yh, z, x, ylo, 1 - core)
    facing = at(yh, z, x, 1 - ylo, core)
    facing_sibling = at(yh, z, x, 1 - ylo, 1 - core)
    to_x = (at(yh, z, xr, ylo, core), at(yh, z, xl, ylo, core))
    to_x_over = at(yh, z, xo, ylo, core)
    to_z = (at(yh, zr, x, ylo, core), at(yh, zl, x, ylo, core))

    def remote(src, dst, ssem, rsem, device):
        return pltpu.make_async_remote_copy(
            src_ref=src, dst_ref=dst, send_sem=ssem, recv_sem=rsem,
            device_id=device, device_id_type=MESH,
        )

    def cotangents():
        for h in range(2):
            yield q_cot.at[:, pl.ds(h * 768, 512)], a2.at[core, h, pl.ds(0, TOK)]
            yield q_cot.at[:, pl.ds(h * 768 + 512, 256)], a1.at[core, h]
            yield k_cot.at[:, pl.ds(h * 512, 512)], a2.at[core, h, pl.ds(TOK, TOK)]

    own_lat = pltpu.make_async_copy(q_lat_hbm, q_lat, local_sem.at[6])
    own_lat.start()
    own_rows = [
        pltpu.make_async_copy(src, dst, local_sem.at[i])
        for i, (src, dst) in enumerate(cotangents())
    ]
    for copy in own_rows:
        copy.start()

    barrier = pltpu.get_barrier_semaphore()
    partners = [to_x[0], to_x[1], to_x_over, to_z[0], to_z[1], facing, facing_sibling, sibling]
    for j in range(1, NYH):
        for c in range(2):
            partners.append(at((yh + j) % NYH, z, x, ylo, c))
    for device in partners:
        pl.semaphore_signal(barrier, inc=1, device_id=device, device_id_type=MESH)

    uq = w_uq[...].astype(jnp.float32)
    uk = w_uk[...].astype(jnp.float32)
    for h in range(2):
        stage1[8 * h : 8 * h + 6] = uq[:, h * 768 : (h + 1) * 768]
        stage1[8 * h + 6 : 8 * h + 8, 0:512] = uk[:, h * 512 : (h + 1) * 512]
        stage1[8 * h + 6 : 8 * h + 8, 512:768] = jnp.zeros((2, 256), jnp.float32)
    y_send[...] = stage1[...].astype(jnp.bfloat16)

    pl.semaphore_wait(barrier, len(partners))

    y_core, y_half = yh % 2, yh // 2
    for j in range(NYH):
        stays = jnp.logical_and(yh == j, y_core == core)

        @pl.when(jnp.logical_not(stays))
        def _(j=j):
            remote(
                y_send, y_land.at[y_half, core], y_ssem.at[j], y_rsem.at[y_half, core],
                at(j, z, x, ylo, y_core),
            ).start()

    mine = y_core == core

    @pl.when(mine)
    def _():
        y_land[y_half, core] = y_send[...]

    give = [
        remote(src, dst, a_send.at[i], a_recv.at[i], sibling)
        for i, (src, dst) in enumerate(cotangents())
    ]
    for copy in give:
        copy.start()

    gain[...] = gain_flat[...].reshape(1, QR)
    own_lat.wait()
    latent = q_lat[...].astype(jnp.float32)
    root_mean = jnp.sqrt(jnp.mean(latent * latent, axis=1, keepdims=True) + norm_eps)
    root[...] = jnp.broadcast_to(root_mean, (TOK, 128))
    for half in range(2):
        columns = pl.ds(pl.multiple_of((core + 2 * half) * SHARE, 128), SHARE)
        normed = q_lat[:, columns].astype(jnp.float32) / root_mean
        gain_normed[half] = (gain[:, columns] * normed).T
    dot_mine[...] = jnp.zeros_like(dot_mine)

    for half in range(2):
        for c in range(2):
            source_yh = core + 2 * half
            local = jnp.logical_and(source_yh == yh, core == c)

            @pl.when(jnp.logical_not(local))
            def _(half=half, c=c, source_yh=source_yh):
                remote(
                    y_send, y_land.at[half, c], y_ssem.at[0], y_rsem.at[half, c],
                    at((yh + 1) % NYH, z, x, ylo, c),
                ).wait_recv()

            piece = y_land[half, c].astype(jnp.float32)
            for h in range(2):
                rank, latents, group = piece[8 * h : 8 * h + 6], piece[8 * h + 6 : 8 * h + 8], 2 * c + h
                stage2[6 * half : 6 * half + 6, group * 512 : group * 512 + 512] = rank[:, 0:512]
                stage2[12 + 2 * half : 14 + 2 * half, group * 512 : group * 512 + 512] = latents[:, 0:512]
                if group < 3:
                    stage1[6 * half : 6 * half + 6, group * 256 : group * 256 + 256] = rank[:, 512:768]
                elif half == 0:
                    stage1[12:16, 0:256] = rank[0:4, 512:768]
                    stage1[12:14, 256:512] = rank[4:6, 512:768]
                else:
                    stage1[14:16, 256:512] = rank[0:2, 512:768]
                    stage1[12:16, 512:768] = rank[2:6, 512:768]

    def rows_of(nx):
        return pl.ds(pl.multiple_of(nx * 16, 16), 16)

    w1[z, rows_of(x), 0:768] = stage1[...].astype(jnp.bfloat16)
    w1[z, rows_of(x), 768:C1] = stage2[:, C2:2048].astype(jnp.bfloat16)
    w2[z, rows_of(x), :] = stage2[:, 0:C2].astype(jnp.bfloat16)

    def ring2(way, block):
        src = w2.at[block, rows_of(x)]
        return remote(src, src, z2_send.at[0], z2_recv.at[block], to_z[way])

    def cross(way, block, half, first):
        src = w2.at[block, rows_of(x), pl.ds(half * HALF, HALF)]
        sem = x2_first.at[way, block] if first else x2_rest.at[block]
        return remote(src, src, x2_send.at[0], sem, to_x[way])

    def start_cross(block):
        for way in range(2):
            cross(way, block, way, True).start()
        for way in range(2):
            cross(way, block, 1 - way, False).start()

    def ring1(way, block, nx):
        src = w1.at[block, rows_of(nx)]
        return remote(src, src, z1_send.at[0], z1_recv.at[block, nx], to_z[way])

    ring2(0, z).start()
    ring2(1, z).start()
    src1 = w1.at[z, rows_of(x)]
    for k, device in enumerate((to_x[0], to_x[1], to_x_over)):
        remote(src1, src1, x1_send.at[0], x1_recv.at[x], device).start()
    ring1(0, z, x).start()
    ring1(1, z, x).start()
    start_cross(z)

    for nx in (xr, xl, xo):
        dst = w1.at[z, rows_of(nx)]
        remote(dst, dst, x1_send.at[0], x1_recv.at[nx], to_x_over).wait_recv()
        ring1(0, z, nx).start()
        ring1(1, z, nx).start()

    for i in range(6):
        own_rows[i].wait()
        give[i].wait_recv()

    def multiply(block_a, block_b):
        def both(ref, start, size):
            return jnp.concatenate(
                [ref[block_a, :, start : start + size], ref[block_b, :, start : start + size]], axis=0
            )

        def times(left, right):
            return lax.dot_general(
                left, right, (((1,), (1,)), ((), ())), preferred_element_type=jnp.float32
            )

        total = times(both(w2, 0, 512), a2[0, 0])
        for t in range(1, 3):
            total = total + times(both(w2, t * 512, 512), a2[t // 2, t % 2])
        last = jnp.concatenate([both(w2, 1536, 256), both(w1, 768, 256)], axis=1)
        total = total + times(last, a2[1, 1])
        products[:, 0 : 2 * TOK] = total
        firsts = [both(w1, t * 256, 256) for t in range(3)]
        total = times(firsts[0], a1[0, 0]) + times(firsts[1], a1[0, 1]) + times(firsts[2], a1[1, 0])
        products[:, 0:TOK] += total
        for t in range(3):
            products[:, (2 + t) * TOK : (3 + t) * TOK] = times(firsts[t], a1[1, 1])
        for base in range(0, 128, 16):
            for t in range(3):
                products[base + 4 * t : base + 4 * t + 4, 0:TOK] += products[
                    base + 12 : base + 16, (2 + t) * TOK : (3 + t) * TOK
                ]
        dot = dot_mine[...]
        for g, block in enumerate((block_a, block_b)):
            for half in range(2):
                for nx in range(NX):
                    base = g * 64 + nx * 16
                    part[half, block, 6 * nx : 6 * nx + 6, :] = products[
                        base + 6 * half : base + 6 * half + 6, 0:TOK
                    ]
                    part[half, block, 24 + 2 * nx : 26 + 2 * nx, :] = products[
                        base + 12 + 2 * half : base + 14 + 2 * half, TOK : 2 * TOK
                    ]
            send_part(block).start()
            for half in range(2):
                weighted = (
                    part[half, block, 0:24, :]
                    * gain_normed[half, pl.ds(pl.multiple_of(block * 24, 8), 24), :]
                )
                dot = dot + (weighted[0:8] + weighted[8:16] + weighted[16:24])
        dot_mine[...] = dot

    def send_part(block):
        return remote(
            part.at[1 - ylo, block], part_in.at[block], part_send.at[0], part_recv.at[block], facing
        )

    def cross_pair(d):
        start_cross((z - d + NZ) % NZ)

        @pl.when(d < 8)
        def _():
            start_cross((z + d) % NZ)

    def forward(block):
        for way, nx in ((0, xl), (1, xr)):
            src = w2.at[block, rows_of(nx), pl.ds(way * HALF, HALF)]
            remote(src, src, fwd_send.at[0], x2_first.at[way, block], to_x[way]).wait_recv()
            remote(src, src, fwd_send.at[0], x2_rest.at[block], to_x[way]).start()

    def ring1_unit(unit):
        step_at, k = unit // 4 + 1, unit % 4
        nx = jnp.where(k == 0, x, jnp.where(k == 1, xr, jnp.where(k == 2, xl, xo)))
        behind, ahead = (z - step_at + NZ) % NZ, (z + step_at) % NZ
        ring1(0, behind, nx).wait_recv()

        @pl.when(step_at < 8)
        def _():
            ring1(0, behind, nx).start()
            ring1(1, ahead, nx).wait_recv()

        @pl.when(step_at < 7)
        def _():
            ring1(1, ahead, nx).start()

    def step(i, carry):
        behind, ahead = (z - i + NZ) % NZ, (z + i) % NZ

        @pl.when(i <= 8)
        def _():
            ring2(0, behind).wait_recv()

            @pl.when(i < 8)
            def _():
                ring2(0, behind).start()
                ring2(1, ahead).wait_recv()

            @pl.when(i < 7)
            def _():
                ring2(1, ahead).start()

            cross_pair(i)
            for k in range(3):
                ring1_unit(3 * i - 3 + k)

        @pl.when(i >= 9)
        def _():
            for k in range(4):
                ring1_unit(4 * i - 12 + k)

        @pl.when(i <= 9)
        def _():
            forward((z - i + 1 + NZ) % NZ)

        @pl.when(jnp.logical_and(i >= 2, i <= 8))
        def _():
            forward((z + i - 1) % NZ)

        @pl.when(i >= 3)
        def _():
            d = i - 2
            block_a = (z - d + NZ) % NZ
            block_b = jnp.where(d == 8, z, (z + d) % NZ)
            for block in (block_a, block_b):
                dst = w2.at[block, :, pl.ds(0, HALF)]
                remote(dst, dst, x2_send.at[0], x2_rest.at[block], to_x[0]).wait_recv()
            multiply(block_a, block_b)

        return carry

    lax.fori_loop(1, 11, step, 0)

    dot_in[head] = dot_mine[...]
    for device in (facing, facing_sibling, sibling):
        remote(dot_mine, dot_in.at[head], dot_send.at[0], dot_recv.at[head], device).start()

    for j in range(NYH):
        stays = jnp.logical_and(yh == j, y_core == core)

        @pl.when(jnp.logical_not(stays))
        def _(j=j):
            remote(
                y_send, y_land.at[y_half, core], y_ssem.at[j], y_rsem.at[y_half, core],
                at(j, z, x, ylo, y_core),
            ).wait_send()

    for copy in give:
        copy.wait_send()

    def sent(ref, sem):
        remote(ref, ref, sem.at[0], dot_recv.at[0], facing).wait_send()

    sent(w1.at[0, pl.ds(0, 48)], x1_send)
    sent(w1.at[pl.ds(0, NZ - 1)], z1_send)
    sent(w2.at[pl.ds(0, NZ - 1), pl.ds(0, 16)], z2_send)
    sent(w2.at[:, pl.ds(0, 32)], x2_send)
    sent(w2.at[:, pl.ds(0, 16)], fwd_send)

    for k in range(1, 4):
        other = (head + k) % 4
        remote(dot_mine, dot_in.at[other], dot_send.at[0], dot_recv.at[other], sibling).wait_recv()
    dots = dot_in[0] + dot_in[1] + dot_in[2] + dot_in[3]
    row_dot = jnp.sum(dots, axis=0, keepdims=True) / QR
    row_dot = jnp.broadcast_to(row_dot, (128, TOK)).T[:, 0:1]

    def arrived(block, carry):
        remote(
            part_in.at[block], part_in.at[block], part_send.at[0], part_recv.at[block], facing
        ).wait_recv()
        return carry

    lax.fori_loop(0, NZ, arrived, 0)
    whole = part[ylo] + part_in[...]
    d_normed = whole[:, 0:24, :].reshape(SHARE, TOK).T
    d_latent[...] = whole[:, 24:32, :].reshape(LSHARE, TOK).T.astype(jnp.bfloat16)
    columns = pl.ds(pl.multiple_of(head * SHARE, 128), SHARE)
    root_mean = root[:, 0:1]
    normed = q_lat[:, columns].astype(jnp.float32) / root_mean
    scaled = gain[:, columns] * d_normed
    d_query[...] = ((scaled - normed * row_dot) / root_mean).astype(jnp.bfloat16)
    sent(part_in, part_send)
    sent(dot_in.at[pl.ds(0, 3)], dot_send)


def on_device(q_cot, k_cot, q_latent, q_gain, w_uq, w_uk):
    vmem = pl.BlockSpec(memory_space=pltpu.VMEM)
    hbm = pl.BlockSpec(memory_space=pl.ANY)
    f32, bf16 = jnp.float32, jnp.bfloat16
    dma = pltpu.SemaphoreType.DMA
    return pl.pallas_call(
        kernel,
        out_shape=(
            jax.ShapeDtypeStruct((TOK, SHARE), bf16),
            jax.ShapeDtypeStruct((TOK, LSHARE), bf16),
        ),
        in_specs=[hbm, hbm, hbm, vmem, vmem, vmem],
        out_specs=(vmem, vmem),
        scratch_shapes=[
            pltpu.VMEM((2, 2, TOK, 256), bf16),
            pltpu.VMEM((2, 2, 2 * TOK, 512), bf16),
            pltpu.VMEM((NZ, 64, C1), bf16),
            pltpu.VMEM((NZ, 64, C2), bf16),
            pltpu.VMEM((2, 2, 16, 768), bf16),
            pltpu.VMEM((16, 768), bf16),
            pltpu.VMEM((16, 768), f32),
            pltpu.VMEM((16, 2048), f32),
            pltpu.VMEM((TOK, QR), bf16),
            pltpu.VMEM((TOK, 128), f32),
            pltpu.VMEM((2, SHARE, TOK), f32),
            pltpu.VMEM((128, 5 * TOK), f32),
            pltpu.VMEM((2, NZ, 32, TOK), f32),
            pltpu.VMEM((NZ, 32, TOK), f32),
            pltpu.VMEM((8, TOK), f32),
            pltpu.VMEM((4, 8, TOK), f32),
            pltpu.VMEM((1, QR), f32),
            dma((7,)),
            dma((6,)),
            dma((6,)),
            dma((4,)),
            dma((2, 2)),
            dma((1,)),
            dma((NX,)),
            dma((1,)),
            dma((NZ, NX)),
            dma((1,)),
            dma((NZ,)),
            dma((1,)),
            dma((2, NZ)),
            dma((NZ,)),
            dma((1,)),
            dma((1,)),
            dma((NZ,)),
            dma((1,)),
            dma((4,)),
        ],
        compiler_params=pltpu.CompilerParams(
            collective_id=0, has_side_effects=True, vmem_limit_bytes=62 * 2**20
        ),
        name="latent_backward",
    )(q_cot, k_cot, q_latent, q_gain, w_uq, w_uk)


def solution(mesh):
    return jax.shard_map(
        on_device,
        mesh=mesh,
        in_specs=(
            P("dp", "head"),
            P("dp", "head"),
            P("dp", None),
            P(),
            P("dp", "head"),
            P("dp", "head"),
        ),
        out_specs=(P("dp", "head"), P("dp", "head")),
        check_vma=False,
    )
```

time: 85.2 us -> 79.1 us (0.928)
  local copies, waits for them, and re-layouts: 6.06 us -> 2.29 us
  Pallas kernels: 78 us -> 76 us
    unnamed x12 -> x4, local copies, waits for them, and re-layouts: 5.35 us -> 2.29 us
    pallas_call x1, Pallas kernels: 78 us -> 76 us  [on_device(): pl.pallas_call(kernel, out_shape=(jax.ShapeDtypeStruct((TOK, SHARE), bf16...]
where the time goes in v2:
time: 79.1 us; the launch traced here: 78.9 us
  Pallas kernels  76 us (96%)
  local copies, waits for them, and re-layouts  2.29 us (3%)
    pallas_call x1, Pallas kernels, on_device(): pl.pallas_call(kernel, out_shape=(jax.ShapeDtypeStruct((TOK, SHARE), bf16...  76 us
    unnamed x4, local copies, waits for them, and re-layouts  2.29 us

profile of v2, /device:TPU:1, one launch (start us, length us, event | category | flops | bytes accessed | tf_op | source)
XLA Modules:
  0.0 78.9 jit_solution(14164880172406848765)
XLA Ops:
  0.6 76.0 %latent_backward.1 = (bf16[256,384]{1,0:T(8,128)(2,1)}, bf16[256,128]{1,0:T(8,128)(2,1)}) custom-call(bf16[256,1536]{1,0:T(8,128)(2,1)} %q_cot.1, bf16[256,1024]{1,0:T(8,128)(2,1)} %k_cot.1, bf16[256,1536]{1,0:T(8,128)(2,1)} %q_lat_hbm.1, f32[1536]{0:T(1024)} %gain_flat.1, bf16[6,1536]{1,0:T(8,128)(2,1)} %w_uq.1, bf16[2,1024]{1,0:T(2,128)(2,1)} %w_uk.1), custom_call_target="tpu_custom_call" | custom-call | tf_op jit(solution)/shard_map/latent_backward/pallas_call | solution.py:374
  76.6 0.0 copy-start
  76.6 1.7 %copy.10 = bf16[256,384]{1,0:T(8,128)(2,1)} copy(bf16[256,384]{1,0:T(8,128)(2,1)} %get-tuple-element.4) | data formatting | bytes 393216
  78.3 0.0 copy-done
  78.3 0.6 copy.11
Async XLA Ops:
  76.6 1.7 %copy-start = (bf16[256,128]{1,0:T(8,128)(2,1)S(1)}, bf16[256,128]{1,0:T(8,128)(2,1)}, u32[]{:S(2)}) copy-start(bf16[256,128]{1,0:T(8,128)(2,1)} %get-tuple-element.5) | copy-start | bytes 196612

commit v3 on v2

--- a/solution.py
+++ b/solution.py
@@ -153,6 +153,10 @@
         src = w2.at[block, rows_of(x)]
         return remote(src, src, z2_send.at[0], z2_recv.at[block], to_z[way])
 
+    def ring2_half(way, block):
+        src = w2.at[block, rows_of(x), pl.ds(way * HALF, HALF)]
+        return remote(src, src, z2_send.at[0], z2_recv.at[block], to_z[way])
+
     def cross(way, block, half, first):
         src = w2.at[block, rows_of(x), pl.ds(half * HALF, HALF)]
         sem = x2_first.at[way, block] if first else x2_rest.at[block]
@@ -187,7 +191,7 @@
         own_rows[i].wait()
         give[i].wait_recv()
 
-    def multiply(block_a, block_b):
+    def multiply(block_a, block_b, second):
         def both(ref, start, size):
             return jnp.concatenate(
                 [ref[block_a, :, start : start + size], ref[block_b, :, start : start + size]], axis=0
@@ -214,8 +218,8 @@
                 products[base + 4 * t : base + 4 * t + 4, 0:TOK] += products[
                     base + 12 : base + 16, (2 + t) * TOK : (3 + t) * TOK
                 ]
-        dot = dot_mine[...]
-        for g, block in enumerate((block_a, block_b)):
+
+        def give_out(g, block):
             for half in range(2):
                 for nx in range(NX):
                     base = g * 64 + nx * 16
@@ -226,25 +230,25 @@
                         base + 12 + 2 * half : base + 14 + 2 * half, TOK : 2 * TOK
                     ]
             send_part(block).start()
+            dot = dot_mine[...]
             for half in range(2):
                 weighted = (
                     part[half, block, 0:24, :]
                     * gain_normed[half, pl.ds(pl.multiple_of(block * 24, 8), 24), :]
                 )
                 dot = dot + (weighted[0:8] + weighted[8:16] + weighted[16:24])
-        dot_mine[...] = dot
+            dot_mine[...] = dot
+
+        give_out(0, block_a)
+
+        @pl.when(second)
+        def _():
+            give_out(1, block_b)
 
     def send_part(block):
         return remote(
             part.at[1 - ylo, block], part_in.at[block], part_send.at[0], part_recv.at[block], facing
         )
-
-    def cross_pair(d):
-        start_cross((z - d + NZ) % NZ)
-
-        @pl.when(d < 8)
-        def _():
-            start_cross((z + d) % NZ)
 
     def forward(block):
         for way, nx in ((0, xl), (1, xr)):
@@ -258,12 +262,15 @@
         behind, ahead = (z - step_at + NZ) % NZ, (z + step_at) % NZ
         ring1(0, behind, nx).wait_recv()
 
+        @pl.when(jnp.logical_or(step_at < 7, jnp.logical_and(step_at == 7, k < 2)))
+        def _():
+            ring1(0, behind, nx).start()
+
         @pl.when(step_at < 8)
         def _():
-            ring1(0, behind, nx).start()
             ring1(1, ahead, nx).wait_recv()
 
-        @pl.when(step_at < 7)
+        @pl.when(jnp.logical_or(step_at < 7, jnp.logical_and(step_at == 7, k >= 2)))
         def _():
             ring1(1, ahead, nx).start()
 
@@ -274,16 +281,40 @@
         def _():
             ring2(0, behind).wait_recv()
 
-            @pl.when(i < 8)
+            @pl.when(i < 7)
             def _():
                 ring2(0, behind).start()
-                ring2(1, ahead).wait_recv()
+
+            @pl.when(i == 7)
+            def _():
+                ring2_half(0, behind).start()
+
+            start_cross(behind)
+
+        @pl.when(i < 8)
+        def _():
+            ring2(1, ahead).wait_recv()
 
             @pl.when(i < 7)
             def _():
                 ring2(1, ahead).start()
 
-            cross_pair(i)
+            @pl.when(i == 7)
+            def _():
+                ring2_half(1, ahead).start()
+
+            start_cross(ahead)
+
+        @pl.when(i <= 9)
+        def _():
+            forward((z - i + 1 + NZ) % NZ)
+
+        @pl.when(jnp.logical_and(i >= 2, i <= 8))
+        def _():
+            forward((z + i - 1) % NZ)
+
+        @pl.when(i <= 8)
+        def _():
             for k in range(3):
                 ring1_unit(3 * i - 3 + k)
 
@@ -292,23 +323,23 @@
             for k in range(4):
                 ring1_unit(4 * i - 12 + k)
 
-        @pl.when(i <= 9)
-        def _():
-            forward((z - i + 1 + NZ) % NZ)
-
-        @pl.when(jnp.logical_and(i >= 2, i <= 8))
-        def _():
-            forward((z + i - 1) % NZ)
-
-        @pl.when(i >= 3)
+        @pl.when(i >= 2)
         def _():
             d = i - 2
-            block_a = (z - d + NZ) % NZ
-            block_b = jnp.where(d == 8, z, (z + d) % NZ)
-            for block in (block_a, block_b):
+            block_a, block_b = (z - d + NZ) % NZ, (z + d) % NZ
+            second = jnp.logical_and(d >= 1, d < 8)
+
+            def rest(block):
                 dst = w2.at[block, :, pl.ds(0, HALF)]
                 remote(dst, dst, x2_send.at[0], x2_rest.at[block], to_x[0]).wait_recv()
-            multiply(block_a, block_b)
+
+            rest(block_a)
+
+            @pl.when(second)
+            def _():
+                rest(block_b)
+
+            multiply(block_a, block_b, second)
 
         return carry
 
@@ -366,17 +397,23 @@
     sent(dot_in.at[pl.ds(0, 3)], dot_send)
 
 
+def hand_over(query_in, latent_in, query_out, latent_out):
+    query_out[...] = query_in[...]
+    latent_out[...] = latent_in[...]
+
+
 def on_device(q_cot, k_cot, q_latent, q_gain, w_uq, w_uk):
     vmem = pl.BlockSpec(memory_space=pltpu.VMEM)
     hbm = pl.BlockSpec(memory_space=pl.ANY)
     f32, bf16 = jnp.float32, jnp.bfloat16
     dma = pltpu.SemaphoreType.DMA
-    return pl.pallas_call(
+    out_shape = (
+        jax.ShapeDtypeStruct((TOK, SHARE), bf16),
+        jax.ShapeDtypeStruct((TOK, LSHARE), bf16),
+    )
+    results = pl.pallas_call(
         kernel,
-        out_shape=(
-            jax.ShapeDtypeStruct((TOK, SHARE), bf16),
-            jax.ShapeDtypeStruct((TOK, LSHARE), bf16),
-        ),
+        out_shape=out_shape,
         in_specs=[hbm, hbm, hbm, vmem, vmem, vmem],
         out_specs=(vmem, vmem),
         scratch_shapes=[
@@ -422,6 +459,9 @@
         ),
         name="latent_backward",
     )(q_cot, k_cot, q_latent, q_gain, w_uq, w_uk)
+    return pl.pallas_call(
+        hand_over, out_shape=out_shape, in_specs=[vmem, vmem], out_specs=(vmem, vmem), name="hand_over"
+    )(*results)
 
 
 def solution(mesh):

time: 79.1 us -> 76.9 us (0.972)
  local copies, waits for them, and re-layouts: 2.29 us -> 0 us
    unnamed x4 -> x0, local copies, waits for them, and re-layouts: 2.29 us -> none
    pallas_call x1 -> x2, Pallas kernels: 76 us -> 76 us  [the longest x1 74.4 us: on_device(): pl.pallas_call(kernel, out_shape=out_shape, in_specs=[hbm, hbm, hbm, vmem...]
where the time goes in v3:
time: 76.9 us; the launch traced here: 76.7 us
  Pallas kernels  76 us (99%)
    pallas_call x1, Pallas kernels, on_device(): pl.pallas_call(kernel, out_shape=out_shape, in_specs=[hbm, hbm, hbm, vmem...  74.4 us
    pallas_call x1, Pallas kernels, on_device(): pl.pallas_call(hand_over, out_shape=out_shape, in_specs=[vmem, vmem], out...  1.65 us

profile of v3, /device:TPU:1, one launch (start us, length us, event | category | flops | bytes accessed | tf_op | source)
XLA Modules:
  0.0 76.7 jit_solution(4499983799250537042)
XLA Ops:
  0.6 74.4 %latent_backward.1 = (bf16[256,384]{1,0:T(8,128)(2,1)}, bf16[256,128]{1,0:T(8,128)(2,1)}) custom-call(bf16[256,1536]{1,0:T(8,128)(2,1)} %q_cot.1, bf16[256,1024]{1,0:T(8,128)(2,1)} %k_cot.1, bf16[256,1536]{1,0:T(8,128)(2,1)} %q_lat_hbm.1, f32[1536]{0:T(1024)} %gain_flat.1, bf16[6,1536]{1,0:T(8,128)(2,1)} %w_uq.1, bf16[2,1024]{1,0:T(2,128)(2,1)} %w_uk.1), custom_call_target="tpu_custom_call" | custom-call | tf_op jit(solution)/shard_map/latent_backward/pallas_call | solution.py:414
  75.0 1.6 %hand_over.1 = (bf16[256,384]{1,0:T(8,128)(2,1)}, bf16[256,128]{1,0:T(8,128)(2,1)}) custom-call(bf16[256,384]{1,0:T(8,128)(2,1)} %get-tuple-element.4.query_in, bf16[256,128]{1,0:T(8,128)(2,1)} %get-tuple-element.5.latent_in), custom_call_target="tpu_custom_call" | custom-call | tf_op jit(solution)/shard_map/hand_over/pallas_call | solution.py:462

commit v4 on v3

--- a/solution.py
+++ b/solution.py
@@ -305,14 +305,6 @@
 
             start_cross(ahead)
 
-        @pl.when(i <= 9)
-        def _():
-            forward((z - i + 1 + NZ) % NZ)
-
-        @pl.when(jnp.logical_and(i >= 2, i <= 8))
-        def _():
-            forward((z + i - 1) % NZ)
-
         @pl.when(i <= 8)
         def _():
             for k in range(3):
@@ -322,6 +314,14 @@
         def _():
             for k in range(4):
                 ring1_unit(4 * i - 12 + k)
+
+        @pl.when(i <= 9)
+        def _():
+            forward((z - i + 1 + NZ) % NZ)
+
+        @pl.when(jnp.logical_and(i >= 2, i <= 8))
+        def _():
+            forward((z + i - 1) % NZ)
 
         @pl.when(i >= 2)
         def _():
@@ -397,9 +397,17 @@
     sent(dot_in.at[pl.ds(0, 3)], dot_send)
 
 
-def hand_over(query_in, latent_in, query_out, latent_out):
-    query_out[...] = query_in[...]
-    latent_out[...] = latent_in[...]
+def hand_over(query_in, latent_in, query_out, latent_out, query, latent, sem_in, sem_out):
+    ways = ((query_in, query, query_out), (latent_in, latent, latent_out))
+    arriving = [pltpu.make_async_copy(a, b, sem_in.at[i]) for i, (a, b, _) in enumerate(ways)]
+    leaving = [pltpu.make_async_copy(b, c, sem_out.at[i]) for i, (_, b, c) in enumerate(ways)]
+    for copy in arriving:
+        copy.start()
+    for copy, onward in zip(arriving, leaving):
+        copy.wait()
+        onward.start()
+    for copy in leaving:
+        copy.wait()
 
 
 def on_device(q_cot, k_cot, q_latent, q_gain, w_uq, w_uk):
@@ -460,7 +468,17 @@
         name="latent_backward",
     )(q_cot, k_cot, q_latent, q_gain, w_uq, w_uk)
     return pl.pallas_call(
-        hand_over, out_shape=out_shape, in_specs=[vmem, vmem], out_specs=(vmem, vmem), name="hand_over"
+        hand_over,
+        out_shape=out_shape,
+        in_specs=[hbm, hbm],
+        out_specs=(hbm, hbm),
+        scratch_shapes=[
+            pltpu.VMEM((TOK, SHARE), bf16),
+            pltpu.VMEM((TOK, LSHARE), bf16),
+            dma((2,)),
+            dma((2,)),
+        ],
+        name="hand_over",
     )(*results)
 
 

time: 76.9 us -> 76.9 us (level)
  no operation moved by 1% of the time
where the time goes in v4:
time: 76.9 us; the launch traced here: 76.6 us
  Pallas kernels  76 us (99%)
    pallas_call x1, Pallas kernels, on_device(): pl.pallas_call(kernel, out_shape=out_shape, in_specs=[hbm, hbm, hbm, vmem...  74.3 us
    pallas_call x1, Pallas kernels, on_device(): pl.pallas_call(hand_over, out_shape=out_shape, in_specs=[hbm, hbm], out_s...  1.65 us

profile of v4, /device:TPU:1, one launch (start us, length us, event | category | flops | bytes accessed | tf_op | source)
XLA Modules:
  0.0 76.6 jit_solution(14366346266840756864)
XLA Ops:
  0.6 74.3 %latent_backward.1 = (bf16[256,384]{1,0:T(8,128)(2,1)}, bf16[256,128]{1,0:T(8,128)(2,1)}) custom-call(bf16[256,1536]{1,0:T(8,128)(2,1)} %q_cot.1, bf16[256,1024]{1,0:T(8,128)(2,1)} %k_cot.1, bf16[256,1536]{1,0:T(8,128)(2,1)} %q_lat_hbm.1, f32[1536]{0:T(1024)} %gain_flat.1, bf16[6,1536]{1,0:T(8,128)(2,1)} %w_uq.1, bf16[2,1024]{1,0:T(2,128)(2,1)} %w_uk.1), custom_call_target="tpu_custom_call" | custom-call | tf_op jit(solution)/shard_map/latent_backward/pallas_call | solution.py:422
  75.0 1.7 %hand_over.1 = (bf16[256,384]{1,0:T(8,128)(2,1)}, bf16[256,128]{1,0:T(8,128)(2,1)}) custom-call(bf16[256,384]{1,0:T(8,128)(2,1)} %get-tuple-element.4.query_in, bf16[256,128]{1,0:T(8,128)(2,1)} %get-tuple-element.5.latent_in), custom_call_target="tpu_custom_call" | custom-call | tf_op jit(solution)/shard_map/hand_over/pallas_call | solution.py:470
